TPU v7x, 32 devices: a whole 2x2x4 slice. The times are simulated.
32 devices in a mesh: grp: 2 (over y), chan: 4 (over z), tm: 2 (over x), sub: 2 (over core).
Axes of the slice: x: 2, y: 2, z: 4, core: 2. Of those that a mesh axis runs over, the one named last changes fastest.
Arguments:
- traces: bfloat16 [1024, 4, 4096], P(('grp', 'chan'), 'tm'), parts along dimension 0
- valid: int32 [1024, 4], P(('grp', 'chan'), 'tm'), parts along dimension 0, may hold values from 0 to 1
- source_channel_index: int32 [8, 32], P(('grp', 'sub')), parts along dimension 0, may hold values from 0 to 511, as said below
Outputs:
- stack: float32 [32, 256, 512], P(None, ('grp', 'sub'), ('chan', 'tm')), parts along dimension 1
There are 2 independent parts, one for each index of `grp`. A program takes and returns all parts, laid end to end along the dimension named above; each array names one. Nothing has to cross between parts.
Inputs may be any that keep to these rules, and one draw needn't show every extreme that they name: `source_channel_index`: the 32 channels of one panel are distinct and lie in one block of 128 channels (b * 128 to b * 128 + 127); different panels lie in different blocks.
All inputs are finite; a program needn't handle non-finite values.
Results may differ from a plain program's by a relative error of at most 0.0003.
Values may be sent and summed in bfloat16 or wider, within the bound.
A program may use at most 64 MiB of HBM per device.

v0:
```python
import math

import jax
import jax.numpy as jnp
from jax import lax
from jax.sharding import PartitionSpec as P

LAGS = 32


def from_root(array, axis, root):
    mine = lax.axis_index(axis) == root
    return lax.psum(jnp.where(mine, array, jnp.zeros_like(array)), axis)


def shifted_block(src, first, count):
    width = src.shape[-1]
    rows = []
    for lag in range(first, first + count):
        rows.append(jnp.pad(src, ((0, 0), (0, 0), (lag, 0)))[:, :, :width])
    return jnp.stack(rows)


def body(traces, valid, source_channel_index):
    resident_traces = traces.shape[0]
    seg_here = traces.shape[1]
    width = traces.shape[2]
    panels_here = source_channel_index.shape[0]
    per_panel = source_channel_index.shape[1]
    rms_rec = jnp.sqrt(jnp.mean(jnp.square(traces.astype(jnp.float32)), axis=2) + 1e-05)
    rec_mask = valid.astype(jnp.float32)
    owners = source_channel_index[:, 0] // resident_traces
    local_rows = (source_channel_index - owners[:, None] * resident_traces).reshape(-1)
    picked = traces[local_rows].reshape(panels_here, per_panel, seg_here, width)
    pick_mask = valid[local_rows].reshape(panels_here, per_panel, seg_here).astype(jnp.bfloat16)

    def fetch(panel):
        return (
            from_root(picked[panel], "chan", owners[panel]),
            from_root(pick_mask[panel], "chan", owners[panel]),
        )

    fetched = [fetch(panel) for panel in range(panels_here)]
    sources = jnp.stack([item[0] for item in fetched])
    src_flags = jnp.stack([item[1] for item in fetched])
    sources = sources.reshape(panels_here * per_panel, seg_here, width)
    src_mask = src_flags.reshape(panels_here * per_panel, seg_here).astype(jnp.float32)
    rms_src = jnp.sqrt(jnp.mean(jnp.square(sources.astype(jnp.float32)), axis=2) + 1e-05)
    scale = (
        src_mask.T[:, :, None]
        * rec_mask.T[:, None, :]
        / (math.sqrt(width) * rms_src.T[:, :, None] * rms_rec.T[:, None, :])
    )
    group = min(8, LAGS)
    blocks = []
    for start in range(0, LAGS, group):
        lag_shifted = shifted_block(sources, start, group)
        lagged_product = jnp.einsum(
            "lsku,rku->klsr", lag_shifted, traces, preferred_element_type=jnp.float32
        )
        blocks.append(jnp.sum(lagged_product * scale[:, None], axis=0))
    partial_stack_value = jnp.concatenate(blocks, axis=0)
    pair_terms = jnp.dot(src_mask, rec_mask.T, preferred_element_type=jnp.float32)
    total, pairs = (
        lax.psum_scatter(partial_stack_value, "tm", scatter_dimension=2, tiled=True),
        lax.psum_scatter(pair_terms, "tm", scatter_dimension=1, tiled=True),
    )
    return total / jnp.sqrt(jnp.maximum(pairs, 1.0))[None]


def solution(mesh):
    in_specs = (P(("grp", "chan"), "tm", None), P(("grp", "chan"), "tm"), P(("grp", "sub"), None))
    out_specs = P(None, ("grp", "sub"), ("chan", "tm"))
    return jax.shard_map(body, mesh=mesh, in_specs=in_specs, out_specs=out_specs, check_vma=False)
```

profile of v0, /device:TPU:0, one launch (start us, length us, event | category | flops | bytes accessed | tf_op | source)
XLA Modules:
  0.0 146.2 jit_solution(13206774797702084006)
XLA Ops:
  7.4 0.8 multiply_reduce_fusion.2
  8.2 0.8 broadcast_subtract_fusion
  11.0 4.2 %gather_fusion = bf16[64,2,4096]{2,1,0:T(2,128)(2,1)S(1)} fusion(bf16[128,2,4096]{2,1,0:T(2,128)(2,1)} %param.3, s32[1024]{0:T(1024)S(1)} %pad_clamp_fusion), kind=kCustom, calls=%fused_computation | custom fusion | bytes 2097408 | tf_op jit(solution)/shard_map/gather | solution.py:34
  15.3 1.8 %fusion.110 = (bf16[1,32,2,4096]{3,2,1,0:T(2,128)(2,1)}, bf16[1,32,2,4096]{3,2,1,0:T(2,128)(2,1)}) fusion(pred[]{:T(512)S(6)} %eq.9, bf16[64,2,4096]{2,1,0:T(2,128)(2,1)S(1)} %gather_fusion, pred[]{:T(512)S(6)} %eq.8), kind=kLoop, calls=%fused_computation.122 | loop fusion | flops 524288 | bytes 2097154 | tf_op jit(solution)/shard_map/stack | solution.py:44
  17.2 0.8 copy.53
  18.8 13.6 %all-reduce.31 = (bf16[1,32,2]{1,2,0:T(2,128)(2,1)S(1)}, bf16[1,32,2]{1,2,0:T(2,128)(2,1)S(1)}) all-reduce(bf16[1,32,2]{1,2,0:T(2,128)(2,1)S(1)} %bitcast.200, bf16[1,32,2]{1,2,0:T(2,128)(2,1)S(1)} %bitcast.199), channel_id=1, replica_groups=mesh['grp'=2,'chan'=4,'tm'=2,'sub'=2] {'chan'}, use_global_device_ids=true, to_apply=%region_3.4 | all-reduce | flops 128 | bytes 512 | tf_op jit(solution)/shard_map/psum | solution.py:13
  32.5 1.5 %convolution_bitcast_fusion = f32[128,64]{1,0:T(8,128)} fusion(bf16[64,2]{0,1:T(2,128)(2,1)S(1)} %reshape.82, s32[128,2]{0,1:T(2,128)} %param.4), kind=kOutput, calls=%fused_computation.23 | convolution fusion | flops 33024 | bytes 34048
  34.2 0.7 convert_bitcast_fusion.1
  34.9 3.8 %multiply_reduce_fusion = f32[128,2]{1,0:T(8,128)S(1)} fusion(bf16[128,2,4096]{2,1,0:T(2,128)(2,1)} %param.3), kind=kLoop, calls=%fused_computation.8 | loop fusion | flops 3145472 | bytes 2098176 | tf_op jit(solution)/shard_map/reduce_sum | solution.py:30
  38.9 33.4 %all-reduce.35.cloned.1.call-done = (bf16[1,32,2,4096]{3,2,1,0:T(2,128)(2,1)}, bf16[1,32,2,4096]{3,2,1,0:T(2,128)(2,1)}) async-done(((bf16[1,32,2,4096]{3,2,1,0:T(2,128)(2,1)}, bf16[1,32,2,4096]{3,2,1,0:T(2,128)(2,1)}), (bf16[1,32,2,4096]{3,2,1,0:T(2,128)(2,1)}, bf16[1,32,2,4096]{3,2,1,0:T(2,128)(2,1)})) %all-reduce.35.cloned.1.call-update) | async-done | bytes 1048592 | tf_op jit(solution)/shard_map/psum | solution.py:13
  72.3 1.5 constant_dynamic-update-slice_fusion.1
  73.7 1.5 %constant_dynamic-update-slice_fusion = bf16[2,32,2,4096]{3,2,1,0:T(2,128)(2,1)S(1)} fusion(bf16[2,32,2,4096]{3,2,1,0:T(2,128)(2,1)S(1)} %constant_dynamic-update-slice_fusion.1, bf16[1,32,2,4096]{3,2,1,0:T(2,128)(2,1)} %get-tuple-element.10), kind=kLoop, calls=%fused_computation.124 | loop fusion | bytes 1048576 | tf_op jit(solution)/shard_map/stack | solution.py:44
  75.3 1.2 multiply_reduce_fusion.1
  77.2 2.3 %fusion.62 = (bf16[8,64,2,4096]{3,1,2,0:T(8,128)(2,1)S(1)}, bf16[8,64,2,4096]{3,1,2,0:T(8,128)(2,1)}, bf16[8,64,2,4096]{3,1,2,0:T(8,128)(2,1)}) fusion(bf16[64,2,4096]{2,0,1:T(8,128)(2,1)S(1)} %bitcast.172), kind=kLoop, calls=%fused_computation.70 | loop fusion | bytes 4194304
  82.3 2.4 %fusion.29 = f32[8,64,128]{2,1,0:T(8,128)S(1)} fusion(bf16[8,64,2,4096]{3,1,0,2:T(8,128)(2,1)S(1)} %fusion.60, bf16[128,2,4096,1]{2,1,0,3:T(2,128)(2,1)S(1)} %bitcast.188, f32[2,64,128]{2,1,0:T(8,128)S(1)} %multiply_divide_fusion), kind=kOutput, calls=%fused_computation.19 | convolution fusion | flops 1073938432 | bytes 10813440 | tf_op jit(solution)/shard_map/lsku,rku->klsr/dot_general | solution.py:58
  84.7 2.4 %fusion.64 = (bf16[8,64,2,4096]{3,1,2,0:T(8,128)(2,1)S(1)}, bf16[8,64,2,4096]{3,1,2,0:T(8,128)(2,1)}, bf16[8,64,2,4096]{3,1,2,0:T(8,128)(2,1)}) fusion(bf16[8,64,2,4096]{3,1,2,0:T(8,128)(2,1)S(1)} %get-tuple-element.32, bf16[64,2,4096]{2,0,1:T(8,128)(2,1)S(1)} %bitcast.180, bf16[8,64,2,4096]{3,1,2,0:T(8,128)(2,1)} %get-tuple-element.33, ...), kind=kLoop, calls=%fused_computation.72 | loop fusion | bytes 4194304
  87.1 2.2 %fusion.66 = (bf16[8,64,2,4096]{3,1,2,0:T(8,128)(2,1)S(1)}, bf16[8,64,2,4096]{3,1,2,0:T(8,128)(2,1)}, bf16[8,64,2,4096]{3,1,2,0:T(8,128)(2,1)}) fusion(bf16[8,64,2,4096]{3,1,2,0:T(8,128)(2,1)S(1)} %get-tuple-element.29, bf16[64,2,4096]{2,0,1:T(8,128)(2,1)S(1)} %bitcast.181, bf16[8,64,2,4096]{3,1,2,0:T(8,128)(2,1)} %get-tuple-element.30, ...), kind=kLoop, calls=%fused_computation.74 | loop fusion | bytes 4194304
  89.3 2.2 %fusion.68 = (bf16[8,64,2,4096]{3,1,2,0:T(8,128)(2,1)S(1)}, bf16[8,64,2,4096]{3,1,2,0:T(8,128)(2,1)}, bf16[8,64,2,4096]{3,1,2,0:T(8,128)(2,1)}) fusion(bf16[8,64,2,4096]{3,1,2,0:T(8,128)(2,1)S(1)} %get-tuple-element.26, bf16[64,2,4096]{2,0,1:T(8,128)(2,1)S(1)} %bitcast.182, bf16[8,64,2,4096]{3,1,2,0:T(8,128)(2,1)} %get-tuple-element.27, ...), kind=kLoop, calls=%fused_computation.76 | loop fusion | bytes 4194304
  91.4 2.2 %fusion.70 = (bf16[8,64,2,4096]{3,1,2,0:T(8,128)(2,1)S(1)}, bf16[8,64,2,4096]{3,1,2,0:T(8,128)(2,1)}, bf16[8,64,2,4096]{3,1,2,0:T(8,128)(2,1)}) fusion(bf16[8,64,2,4096]{3,1,2,0:T(8,128)(2,1)S(1)} %get-tuple-element.23, bf16[64,2,4096]{2,0,1:T(8,128)(2,1)S(1)} %bitcast.183, bf16[8,64,2,4096]{3,1,2,0:T(8,128)(2,1)} %get-tuple-element.24, ...), kind=kLoop, calls=%fused_computation.78 | loop fusion | bytes 4194304
  93.7 2.2 %fusion.72 = (bf16[8,64,2,4096]{3,1,2,0:T(8,128)(2,1)S(1)}, bf16[8,64,2,4096]{3,1,2,0:T(8,128)(2,1)}, bf16[8,64,2,4096]{3,1,2,0:T(8,128)(2,1)}) fusion(bf16[8,64,2,4096]{3,1,2,0:T(8,128)(2,1)S(1)} %get-tuple-element.20, bf16[64,2,4096]{2,0,1:T(8,128)(2,1)S(1)} %bitcast.184, bf16[8,64,2,4096]{3,1,2,0:T(8,128)(2,1)} %get-tuple-element.21, ...), kind=kLoop, calls=%fused_computation.80 | loop fusion | bytes 4194304
  95.9 2.2 %fusion.74 = (bf16[8,64,2,4096]{3,1,2,0:T(8,128)(2,1)S(1)}, bf16[8,64,2,4096]{3,1,2,0:T(8,128)(2,1)}, bf16[8,64,2,4096]{3,1,2,0:T(8,128)(2,1)}) fusion(bf16[8,64,2,4096]{3,1,2,0:T(8,128)(2,1)S(1)} %get-tuple-element.17, bf16[64,2,4096]{2,0,1:T(8,128)(2,1)S(1)} %bitcast.185, bf16[8,64,2,4096]{3,1,2,0:T(8,128)(2,1)} %get-tuple-element.18, ...), kind=kLoop, calls=%fused_computation.82 | loop fusion | bytes 4194304
  98.0 2.2 %fusion.76 = (bf16[8,64,2,4096]{3,1,2,0:T(8,128)(2,1)S(1)}, bf16[8,64,2,4096]{3,1,2,0:T(8,128)(2,1)}, bf16[8,64,2,4096]{3,1,2,0:T(8,128)(2,1)}) fusion(bf16[8,64,2,4096]{3,1,2,0:T(8,128)(2,1)S(1)} %get-tuple-element.14, bf16[64,2,4096]{2,0,1:T(8,128)(2,1)S(1)} %bitcast.186, bf16[8,64,2,4096]{3,1,2,0:T(8,128)(2,1)} %get-tuple-element.15, ...), kind=kLoop, calls=%fused_computation.84 | loop fusion | bytes 4194304 | tf_op jit(solution)/shard_map/stack | solution.py:21
  100.2 2.4 %fusion.42 = f32[8,64,128]{2,1,0:T(8,128)S(1)} fusion(bf16[128,2,4096,1]{2,1,0,3:T(2,128)(2,1)S(1)} %bitcast.189, bf16[8,64,2,4096]{3,1,2,0:T(8,128)(2,1)S(1)} %get-tuple-element.11, f32[2,64,128]{2,1,0:T(8,128)S(1)} %multiply_divide_fusion), kind=kOutput, calls=%fused_computation.22 | convolution fusion | flops 1073938432 | bytes 10813440 | tf_op jit(solution)/shard_map/lsku,rku->klsr/dot_general | solution.py:58
  102.7 1.0 slice-done.1
  103.7 2.4 %fusion.32 = f32[8,64,128]{2,1,0:T(8,128)S(1)} fusion(bf16[128,2,4096,1]{2,1,0,3:T(2,128)(2,1)S(1)} %bitcast.190, bf16[8,64,2,4096]{3,1,2,0:T(8,128)(2,1)S(1)} %bitcast.195, f32[2,64,128]{2,1,0:T(8,128)S(1)} %multiply_divide_fusion), kind=kOutput, calls=%fused_computation.20 | convolution fusion | flops 1073938432 | bytes 10813440 | tf_op jit(solution)/shard_map/lsku,rku->klsr/dot_general | solution.py:58
  106.1 6.2 %fusion.37 = f32[8,64,128]{2,1,0:T(8,128)S(1)} fusion(bf16[128,2,4096,1]{2,1,0,3:T(2,128)(2,1)S(1)} %bitcast.191, bf16[8,64,2,4096]{3,1,2,0:T(8,128)(2,1)} %get-tuple-element.13, f32[2,64,128]{2,1,0:T(8,128)S(1)} %multiply_divide_fusion), kind=kOutput, calls=%fused_computation.21 | convolution fusion | flops 1073938432 | bytes 10813440 | tf_op jit(solution)/shard_map/lsku,rku->klsr/dot_general | solution.py:58
  112.4 1.8 %copy.78 = f32[32,64,128]{1,0,2:T(8,128)S(1)} copy(f32[32,64,128]{2,1,0:T(8,128)S(1)} %pad_maximum_fusion) | data formatting | bytes 2097152
  114.2 1.6 %reshape.105 = f32[128,2048]{1,0:T(8,128)} reshape(f32[128,32,64]{2,1,0:T(8,128)S(1)} %bitcast.187) | data formatting | bytes 2097152
  115.9 0.8 copy.81
  116.8 18.8 %reduce-scatter.7.cloned.1.call-done = f32[64,2048]{1,0:T(8,128)} async-done(((f32[128,2048]{1,0:T(8,128)}), f32[64,2048]{1,0:T(8,128)}) %reduce-scatter.7.cloned.1.call-update) | async-done | bytes 524304
  135.6 1.5 reshape.106
  137.7 1.1 broadcast_divide_fusion
  (44 shorter events, 6.3 us)
Async XLA Ops:
  7.4 64.9 %all-reduce.35.cloned.1.call-start = ((), (), s32[]{:S(2)}) async-start(), calls=%async_computation.4 | async-start | bytes 2097152 | tf_op jit(solution)/shard_map/psum | solution.py:13
  17.1 98.8 %reduce-scatter.9.cloned.1.call-start = ((), (), s32[]{:S(2)}) async-start(), calls=%async_computation.3 | async-start | bytes 98304
  34.0 101.6 %reduce-scatter.7.cloned.1.call-start = ((), (), s32[]{:S(2)}) async-start(), calls=%async_computation.2 | async-start | bytes 1572864
  79.5 2.8 %copy-start = (bf16[128,2,4096]{2,1,0:T(2,128)(2,1)S(1)}, bf16[128,2,4096]{2,1,0:T(2,128)(2,1)}, u32[]{:S(2)}) copy-start(bf16[128,2,4096]{2,1,0:T(2,128)(2,1)} %param.3) | copy-start | bytes 6291460
  100.2 2.4 %slice-start = ((s8[8388608]{0:T(1024)(128)(4,1)}), s8[4194304]{0:T(1024)(128)(4,1)S(1)}, s32[]{:S(2)}) async-start(s8[8388608]{0:T(1024)(128)(4,1)} %bitcast.194), calls=%async_computation.5 | async-start | bytes 8388608
  100.2 3.5 %slice-start.1 = ((s8[8388608]{0:T(1024)(128)(4,1)}), s8[4194304]{0:T(1024)(128)(4,1)S(1)}, s32[]{:S(2)}) async-start(s8[8388608]{0:T(1024)(128)(4,1)} %bitcast.194), calls=%async_computation.6 | async-start | bytes 8388608
Sparse Core Ops, SparseCore 0:
  17.2 54.9 all-reduce.34
Sparse Core Ops, SparseCore 1:
  34.1 8.0 reduce-scatter.8
  116.0 19.6 reduce-scatter.6
where the time goes:
time: 147 us; the launch traced here: 146 us
  waiting for transfers between devices  52.3 us (36%)
  local copies, waits for them, and re-layouts  38.2 us (26%)
  between operations  16.4 us (11%)
  matrix products  15 us (10%)
  blocking collectives  13.6 us (9%)
  other arithmetic  10.5 us (7%)
    psum x1, waiting for transfers between devices, from_root(): return lax.psum(jnp.where(mine, array, jnp.zeros_like(array)), axis)  33.4 us
    unnamed x28, local copies, waits for them, and re-layouts  27.6 us
    unnamed x5, waiting for transfers between devices  18.9 us
    psum x1, blocking collectives, from_root(): return lax.psum(jnp.where(mine, array, jnp.zeros_like(array)), axis)  13.6 us
    dot_general x4, matrix products, body(): jnp.einsum('lsku,rku->klsr', lag_shifted, traces, preferred_element_type=...  13.5 us
    gather x1, local copies, waits for them, and re-layouts, body(): picked = traces[local_rows].reshape(panels_here, per_panel, seg_here, width)  4.25 us
    reduce_sum x1, other arithmetic, body(): jnp.mean(jnp.square(traces.astype(jnp.float32)), axis=2) + 1e-05  3.84 us
  transfers between devices with their start and end apart: 3, of which 2 were waited for; matrix products, arithmetic and copies ran while one was open for 35% of the time, Pallas kernels for 0%

commit v1 on v0

--- a/solution.py
+++ b/solution.py
@@ -1,16 +1,43 @@
+import functools
 import math
 
 import jax
 import jax.numpy as jnp
 from jax import lax
+from jax.experimental import pallas as pl
+from jax.experimental.pallas import tpu as pltpu
 from jax.sharding import PartitionSpec as P
 
 LAGS = 32
+SRC_SHIFTS = 8
+REC_SHIFTS = LAGS // SRC_SHIFTS
+LANES = 128
+MESH = pl.DeviceIdType.MESH
 
 
 def from_root(array, axis, root):
-    mine = lax.axis_index(axis) == root
-    return lax.psum(jnp.where(mine, array, jnp.zeros_like(array)), axis)
+    size = lax.axis_size(axis)
+    moving = jnp.where(lax.axis_index(axis) == root, array, jnp.zeros_like(array))
+    total = moving
+    for _ in range(size - 1):
+        moving = lax.ppermute(moving, axis, [(i, (i + 1) % size) for i in range(size)])
+        total = total + moving
+    return total
+
+
+def sum_to_owners(array, axis, dim):
+    size = lax.axis_size(axis)
+    part = array.shape[dim] // size
+    me = lax.axis_index(axis)
+
+    def piece(owner):
+        return lax.dynamic_slice_in_dim(array, owner * part, part, dim)
+
+    total = piece(me)
+    for step in range(1, size):
+        away = [(i, (i + step) % size) for i in range(size)]
+        total = total + lax.ppermute(piece((me + step) % size), axis, away)
+    return total
 
 
 def shifted_block(src, first, count):
@@ -21,7 +48,7 @@
     return jnp.stack(rows)
 
 
-def body(traces, valid, source_channel_index):
+def general_body(traces, valid, source_channel_index):
     resident_traces = traces.shape[0]
     seg_here = traces.shape[1]
     width = traces.shape[2]
@@ -61,14 +88,292 @@
         blocks.append(jnp.sum(lagged_product * scale[:, None], axis=0))
     partial_stack_value = jnp.concatenate(blocks, axis=0)
     pair_terms = jnp.dot(src_mask, rec_mask.T, preferred_element_type=jnp.float32)
-    total, pairs = (
-        lax.psum_scatter(partial_stack_value, "tm", scatter_dimension=2, tiled=True),
-        lax.psum_scatter(pair_terms, "tm", scatter_dimension=1, tiled=True),
+    total = sum_to_owners(partial_stack_value, "tm", 2)
+    pairs = sum_to_owners(pair_terms, "tm", 1)
+    return total / jnp.sqrt(jnp.maximum(pairs, 1.0))[None]
+
+
+def kernel(
+    n_chan, x_ref, idx_ref, val_ref, out_ref,
+    slots, idx_sib, shifted_rec, shifted_src, wrow, vrow, own, xsend, xrecv, fin, finr,
+    idx_sems, z_send, z_recv, s_send, s_recv, x_send, x_recv, f_send, f_recv,
+):
+    segs, resident, width = x_ref.shape
+    per = idx_ref.shape[0] // 2
+    q = resident // 4
+    z = lax.axis_index("chan")
+    x = lax.axis_index("tm")
+    k = lax.axis_index("sub")
+    has_left = z > 0
+    has_right = z < n_chan - 1
+
+    barrier = pltpu.get_barrier_semaphore()
+    pl.semaphore_signal(barrier, inc=1, device_id={"sub": 1 - k}, device_id_type=MESH)
+    pl.semaphore_signal(barrier, inc=1, device_id={"tm": 1 - x}, device_id_type=MESH)
+
+    @pl.when(has_left)
+    def _():
+        pl.semaphore_signal(barrier, inc=1, device_id={"chan": z - 1}, device_id_type=MESH)
+
+    @pl.when(has_right)
+    def _():
+        pl.semaphore_signal(barrier, inc=1, device_id={"chan": z + 1}, device_id_type=MESH)
+
+    pl.semaphore_wait(barrier, 2 + has_left.astype(jnp.int32) + has_right.astype(jnp.int32))
+
+    def remote(src, dst, send, recv, where):
+        return pltpu.make_async_remote_copy(
+            src_ref=src, dst_ref=dst, send_sem=send, recv_sem=recv,
+            device_id=where, device_id_type=MESH,
+        )
+
+    def z_copy(b, right):
+        step = 1 if right else -1
+        part = slots.at[b, k]
+        return remote(part, part, z_send.at[b, int(right)], z_recv.at[b], {"chan": z + step})
+
+    def s_copy(b, seg):
+        part = slots.at[b, seg]
+        return remote(part, part, s_send.at[b], s_recv.at[b], {"sub": 1 - k})
+
+    def x_copy(b):
+        return remote(xsend.at[b], xrecv.at[b], x_send.at[b], x_recv.at[b], {"tm": 1 - x})
+
+    def f_copy(b):
+        return remote(fin.at[b], finr.at[b], f_send.at[b], f_recv.at[b], {"sub": 1 - k})
+
+    idx_copy = remote(idx_ref, idx_sib, idx_sems.at[0], idx_sems.at[1], {"sub": 1 - k})
+    idx_copy.start()
+    idx_copy.wait()
+
+    lane = lax.broadcasted_iota(jnp.int32, (per, resident), 1)
+    sel = jnp.zeros((per, resident), jnp.float32)
+    for ref in (idx_ref, idx_sib):
+        for p in range(2):
+            hit = ref[p * per : (p + 1) * per, :] - z * resident == lane
+            sel = sel + jnp.where(hit, 1.0, 0.0)
+    sel = sel.astype(jnp.bfloat16)
+    tile = 1024
+    for t in range(0, width, tile):
+        slots[z, k, :, t : t + tile] = jnp.dot(
+            sel, x_ref[k, :, t : t + tile], preferred_element_type=jnp.float32
+        ).astype(jnp.bfloat16)
+    slots[z, k, :, width:] = jnp.dot(
+        sel, val_ref[k].astype(jnp.bfloat16), preferred_element_type=jnp.float32
+    ).astype(jnp.bfloat16)
+
+    @pl.when(has_left)
+    def _():
+        z_copy(z, False).start()
+
+    @pl.when(has_right)
+    def _():
+        z_copy(z, True).start()
+
+    s_copy(z, k).start()
+
+    wide = lax.broadcasted_iota(jnp.int32, (q, width), 1)
+    for seg in range(segs):
+        wcols, vcols = [], []
+        for half in range(2):
+            side = x if half == 0 else 1 - x
+            first = pl.multiple_of(side * (2 * q) + k * q, q)
+            rec = x_ref[seg, pl.ds(first, q), :].astype(jnp.float32)
+            flag = val_ref[seg, pl.ds(first, q), :]
+            mean = jnp.sum(rec * rec, axis=1, keepdims=True) * (1.0 / width)
+            w = flag / jnp.sqrt(mean + 1e-05)
+            for h in range(REC_SHIFTS):
+                by = SRC_SHIFTS * h
+                moved = rec
+                if by:
+                    moved = jnp.where(wide < width - by, pltpu.roll(rec, width - by, 1), 0.0)
+                row = (half * REC_SHIFTS + h) * q
+                shifted_rec[seg, row : row + q, :] = moved.astype(jnp.bfloat16)
+                wcols.append(w)
+                vcols.append(flag)
+        wrow[seg] = jnp.concatenate(wcols, axis=0).T[:per]
+        vrow[seg] = jnp.concatenate(vcols, axis=0).T[:per]
+
+    def compute(b):
+        s_copy(b, 1 - k).wait_recv()
+        acc = None
+        pairs = None
+        for seg in range(segs):
+            src = slots[b, seg, :, :width].astype(jnp.float32)
+            flag = slots[b, seg, :, width:].astype(jnp.float32)
+            mean = jnp.sum(src * src, axis=1, keepdims=True) * (1.0 / width)
+            a = flag / (math.sqrt(width) * jnp.sqrt(mean + 1e-05))
+            a = jnp.concatenate([a, a], axis=1)
+            f = jnp.concatenate([flag, flag], axis=1)
+            for j in range(SRC_SHIFTS):
+                moved = src
+                if j:
+                    moved = jnp.where(wide[:per] >= j, pltpu.roll(src, j, 1), 0.0)
+                shifted_src[seg, j * per : (j + 1) * per, :] = moved.astype(jnp.bfloat16)
+            d = lax.dot_general(
+                shifted_src[seg], shifted_rec[seg], (((1,), (1,)), ((), ())),
+                preferred_element_type=jnp.float32,
+            )
+            term = d.reshape(SRC_SHIFTS, per, 2 * LANES) * (a * wrow[seg])[None]
+            pair = f * vrow[seg]
+            acc = term if acc is None else acc + term
+            pairs = pair if pairs is None else pairs + pair
+        rows = SRC_SHIFTS * per
+        own[b, :rows] = acc[:, :, :LANES].reshape(rows, LANES)
+        own[b, rows:] = pairs[:, :LANES]
+        xsend[b, :rows] = acc[:, :, LANES:].reshape(rows, LANES)
+        xsend[b, rows:] = pairs[:, LANES:]
+        x_copy(b).start()
+
+    def finish(b):
+        x_copy(b).wait_recv()
+        rows = SRC_SHIFTS * per
+        total = own[b, :rows] + xrecv[b, :rows]
+        pairs = own[b, rows:] + xrecv[b, rows:]
+        norm = 1.0 / jnp.sqrt(jnp.maximum(pairs, 1.0))
+        fin[b] = (total.reshape(SRC_SHIFTS, per, LANES) * norm[None]).reshape(rows, LANES)
+        f_copy(b).start()
+
+    def final(b):
+        f_copy(b).wait_recv()
+        rows = SRC_SHIFTS * per
+        mine, other = fin[b], finr[b]
+        low = jnp.where(k == 0, mine, other)
+        high = jnp.where(k == 0, other, mine)
+        at = lax.broadcasted_iota(jnp.int32, (rows, LANES), 1)
+        for h in range(REC_SHIFTS):
+            lo = pltpu.roll(low, (LANES - h * q) % LANES, 1) if h else low
+            hi = pltpu.roll(high, (LANES + q - h * q) % LANES, 1) if h != 1 else high
+            both = jnp.where(at < q, lo, hi)[:, : 2 * q]
+            out_ref[b, h * SRC_SHIFTS : (h + 1) * SRC_SHIFTS] = both.reshape(SRC_SHIFTS, per, 2 * q)
+
+    def item(d, way):
+        b = z + d * (2 * way - 1)
+        ok = (b >= 0) & (b < n_chan) & (d >= 0) & ((d > 0) | (way == 0))
+        return b, ok
+
+    @pl.loop(0, n_chan + 2)
+    def _(d):
+        from_left, ok_left = item(d, 0)
+        from_right, ok_right = item(d, 1)
+
+        @pl.when(ok_left & (d > 0))
+        def _():
+            z_copy(from_left, True).wait_recv()
+
+            @pl.when(has_right)
+            def _():
+                z_copy(from_left, True).start()
+
+            s_copy(from_left, k).start()
+
+        @pl.when(ok_right & (d > 0))
+        def _():
+            z_copy(from_right, False).wait_recv()
+
+            @pl.when(has_left)
+            def _():
+                z_copy(from_right, False).start()
+
+            s_copy(from_right, k).start()
+
+        @pl.loop(0, 2)
+        def _(way):
+            b, ok = item(d, way)
+
+            @pl.when(ok)
+            def _():
+                compute(b)
+
+            b1, ok1 = item(d - 1, way)
+
+            @pl.when(ok1)
+            def _():
+                finish(b1)
+
+            b2, ok2 = item(d - 2, way)
+
+            @pl.when(ok2)
+            def _():
+                final(b2)
+
+    @pl.loop(0, n_chan)
+    def _(b):
+        @pl.when(has_left & (b >= z))
+        def _():
+            z_copy(b, False).wait_send()
+
+        @pl.when(has_right & (b <= z))
+        def _():
+            z_copy(b, True).wait_send()
+
+        s_copy(b, k).wait_send()
+        x_copy(b).wait_send()
+        f_copy(b).wait_send()
+
+
+def fast_body(n_chan, traces, valid, source_channel_index):
+    resident, segs, width = traces.shape
+    panels, per = source_channel_index.shape
+    x = jnp.transpose(traces, (1, 0, 2))
+    idx = jnp.broadcast_to(source_channel_index.reshape(-1)[:, None], (panels * per, LANES))
+    val = jnp.broadcast_to(valid.T.astype(jnp.float32)[:, :, None], (segs, resident, LANES))
+    rows = SRC_SHIFTS * per
+    vmem = pl.BlockSpec(memory_space=pltpu.VMEM)
+    dma = pltpu.SemaphoreType.DMA
+    f32, bf16 = jnp.float32, jnp.bfloat16
+    found = pl.pallas_call(
+        functools.partial(kernel, n_chan),
+        out_shape=jax.ShapeDtypeStruct((n_chan, LAGS, per, resident // 2), f32),
+        in_specs=[vmem] * 3,
+        out_specs=vmem,
+        scratch_shapes=[
+            pltpu.VMEM((n_chan, segs, per, width + LANES), bf16),
+            pltpu.VMEM((panels * per, LANES), jnp.int32),
+            pltpu.VMEM((segs, 2 * LANES, width), bf16),
+            pltpu.VMEM((segs, rows, width), bf16),
+            pltpu.VMEM((segs, per, 2 * LANES), f32),
+            pltpu.VMEM((segs, per, 2 * LANES), f32),
+            pltpu.VMEM((n_chan, rows + per, LANES), f32),
+            pltpu.VMEM((n_chan, rows + per, LANES), f32),
+            pltpu.VMEM((n_chan, rows + per, LANES), f32),
+            pltpu.VMEM((n_chan, rows, LANES), f32),
+            pltpu.VMEM((n_chan, rows, LANES), f32),
+            dma((2,)),
+            dma((n_chan, 2)),
+            dma((n_chan,)),
+            dma((n_chan,)),
+            dma((n_chan,)),
+            dma((n_chan,)),
+            dma((n_chan,)),
+            dma((n_chan,)),
+            dma((n_chan,)),
+        ],
+        compiler_params=pltpu.CompilerParams(
+            collective_id=0, has_side_effects=True, vmem_limit_bytes=48 * 1024 * 1024
+        ),
+    )(x, idx, val)
+    owners = source_channel_index[:, 0] // resident
+    return jnp.concatenate(
+        [lax.dynamic_index_in_dim(found, owners[p], 0, keepdims=False) for p in range(panels)], axis=1
     )
-    return total / jnp.sqrt(jnp.maximum(pairs, 1.0))[None]
 
 
 def solution(mesh):
     in_specs = (P(("grp", "chan"), "tm", None), P(("grp", "chan"), "tm"), P(("grp", "sub"), None))
     out_specs = P(None, ("grp", "sub"), ("chan", "tm"))
+    size = mesh.shape
+
+    def body(traces, valid, source_channel_index):
+        panels = source_channel_index.shape[0] * size["sub"]
+        fits = (
+            (size["tm"], size["sub"], traces.shape[1]) == (2, 2, 2)
+            and panels == size["chan"]
+            and traces.shape[0] == LANES
+            and source_channel_index.shape == (2, LANES // REC_SHIFTS)
+        )
+        if fits:
+            return fast_body(size["chan"], traces, valid, source_channel_index)
+        return general_body(traces, valid, source_channel_index)
+
     return jax.shard_map(body, mesh=mesh, in_specs=in_specs, out_specs=out_specs, check_vma=False)

time: 147 us -> 48 us (0.33)
  waiting for transfers between devices: 52.3 us -> 0 us
  Pallas kernels: 0 us -> 36.6 us
  local copies, waits for them, and re-layouts: 38.2 us -> 6.48 us
  matrix products: 15 us -> 0 us
  blocking collectives: 13.6 us -> 0 us
  between operations: 16.4 us -> 3.62 us
  other arithmetic: 10.5 us -> 1.08 us
    pallas_call x0 -> x1, Pallas kernels: none -> 36.6 us  [fast_body(): pl.pallas_call(functools.partial(kernel, n_chan), out_shape=jax.ShapeDtyp...]
    psum x1 -> x0, waiting for transfers between devices: 33.4 us -> none  [from_root(): return lax.psum(jnp.where(mine, array, jnp.zeros_like(array)), axis)]
    unnamed x28 -> x7, local copies, waits for them, and re-layouts: 27.6 us -> 4.28 us
    unnamed x5 -> x0, waiting for transfers between devices: 18.9 us -> none
    psum x1 -> x0, blocking collectives: 13.6 us -> none  [from_root(): return lax.psum(jnp.where(mine, array, jnp.zeros_like(array)), axis)]
    dot_general x4 -> x0, matrix products: 13.5 us -> none  [body(): jnp.einsum('lsku,rku->klsr', lag_shifted, traces, preferred_element_type=...]
    reduce_sum x2 -> x0, other arithmetic: 5 us -> none  [the longest x1 3.84 us: body(): jnp.mean(jnp.square(traces.astype(jnp.float32)), axis=2) + 1e-05]
    gather x2 -> x0, local copies, waits for them, and re-layouts: 4.84 us -> none  [the longest x1 4.25 us: body(): picked = traces[local_rows].reshape(panels_here, per_panel, seg_here, width)]
  transfers between devices with their start and end apart: 3 -> 0, of which waited for: 2 -> 0; matrix products, arithmetic and copies ran while one was open for 35% -> 0% of each run, Pallas kernels for 0% -> 0%
where the time goes in v1:
time: 48 us; the launch traced here: 47.8 us
  Pallas kernels  36.6 us (76%)
  local copies, waits for them, and re-layouts  6.48 us (14%)
  between operations  3.62 us (8%)
  other arithmetic  1.08 us (2%)
    pallas_call x1, Pallas kernels, fast_body(): pl.pallas_call(functools.partial(kernel, n_chan), out_shape=jax.ShapeDtyp...  36.6 us
    unnamed x7, local copies, waits for them, and re-layouts  4.28 us
    squeeze x1, local copies, waits for them, and re-layouts, fast_body(): lax.dynamic_index_in_dim(found, owners[p], 0, keepdims=False)  1.27 us
    concatenate x1, other arithmetic, fast_body(): jnp.concatenate([lax.dynamic_index_in_dim(found, owners[p], 0, keepdims=F...  1.07 us

profile of v1, /device:TPU:0, one launch (start us, length us, event | category | flops | bytes accessed | tf_op | source)
XLA Modules:
  0.0 47.8 jit_solution(7188210710157197666)
XLA Ops:
  0.0 0.0 copy-start.2
  0.0 0.0 copy-start.1
  0.0 2.9 %copy.6 = bf16[128,2,4096]{2,0,1:T(8,128)(2,1)S(1)} copy(bf16[128,2,4096]{2,1,0:T(2,128)(2,1)} %param.3) | data formatting | bytes 4194304 | tf_op args[0]
  3.0 0.0 copy-done.2
  3.0 0.1 broadcast_in_dim.6
  3.0 0.1 broadcast_in_dim.14.idx_ref
  3.1 0.0 copy-done.1
  3.1 0.1 broadcast_in_dim.15.val_ref
  3.2 36.6 %shard_map.37 = f32[4,32,32,64]{3,2,1,0:T(8,128)S(1)} custom-call(bf16[2,128,4096]{2,1,0:T(8,128)(2,1)S(1)} %bitcast.11, s32[64,128]{1,0:T(8,128)S(1)} %broadcast_in_dim.14.idx_ref, f32[2,128,128]{2,1,0:T(8,128)S(1)} %broadcast_in_dim.15.val_ref), custom_call_target="tpu_custom_call" | custom-call | tf_op jit(solution)/shard_map/pallas_call | solution.py:325
  39.8 0.0 copy-start
  39.8 1.3 %copy-done = f32[4,32,32,64]{3,2,1,0:T(8,128)} copy-done((f32[4,32,32,64]{3,2,1,0:T(8,128)}, f32[4,32,32,64]{3,2,1,0:T(8,128)S(1)}, u32[]{:S(2)}) %copy-start) | copy-done | bytes 1048600
  41.2 0.1 slice_reduce_fusion
  41.3 0.6 %fusion = (s32[1]{0:T(128)}, s32[1]{0:T(128)}) fusion(s32[2]{0:T(128)S(1)} %and_select_fusion), kind=kLoop, calls=%fused_computation.10 | loop fusion | bytes 16 | tf_op jit(solution)/shard_map/slice | solution.py:358
  45.4 1.3 %dynamic-slice_bitcast_fusion.1 = (f32[32,32,64]{2,1,0:T(8,128)S(1)}, f32[32,32,64]{2,1,0:T(8,128)S(1)}) fusion(f32[4,32,32,64]{3,2,1,0:T(8,128)} %copy-done, s32[]{:T(128)S(6)} %select_n.13, s32[]{:T(128)S(6)} %select_n.14), kind=kLoop, calls=%fused_computation.3 | loop fusion | bytes 1048584 | tf_op jit(solution)/shard_map/jit(dynamic_index_in_dim)/squeeze | solution.py:358
  46.7 1.1 %pad_maximum_fusion = f32[32,64,64]{2,1,0:T(8,128)} fusion(f32[32,32,64]{2,1,0:T(8,128)S(1)} %get-tuple-element.6, f32[32,32,64]{2,1,0:T(8,128)S(1)} %get-tuple-element.5), kind=kLoop, calls=%fused_computation.1 | loop fusion | flops 131072 | bytes 1048576 | tf_op jit(solution)/shard_map/concatenate | solution.py:357
  (2 shorter events, 0.0 us)
Async XLA Ops:
  0.0 3.0 %copy-start.2 = (s32[2,32]{1,0:T(2,128)S(1)}, s32[2,32]{1,0:T(2,128)}, u32[]{:S(2)}) copy-start(s32[2,32]{1,0:T(2,128)} %param.5) | copy-start | bytes 772
  0.0 3.1 %copy-start.1 = (s32[128,2]{0,1:T(2,128)S(1)}, s32[128,2]{0,1:T(2,128)}, u32[]{:S(2)}) copy-start(s32[128,2]{0,1:T(2,128)} %param.4) | copy-start | bytes 3076
  39.8 1.3 %copy-start = (f32[4,32,32,64]{3,2,1,0:T(8,128)}, f32[4,32,32,64]{3,2,1,0:T(8,128)S(1)}, u32[]{:S(2)}) copy-start(f32[4,32,32,64]{3,2,1,0:T(8,128)S(1)} %shard_map.37) | copy-start | bytes 3145732

commit v2 on v1

--- a/solution.py
+++ b/solution.py
@@ -58,8 +58,11 @@
     rec_mask = valid.astype(jnp.float32)
     owners = source_channel_index[:, 0] // resident_traces
     local_rows = (source_channel_index - owners[:, None] * resident_traces).reshape(-1)
-    picked = traces[local_rows].reshape(panels_here, per_panel, seg_here, width)
-    pick_mask = valid[local_rows].reshape(panels_here, per_panel, seg_here).astype(jnp.bfloat16)
+    chosen = (local_rows[:, None] == jnp.arange(resident_traces)[None, :]).astype(jnp.bfloat16)
+    picked = jnp.einsum("nc,ckt->nkt", chosen, traces, preferred_element_type=jnp.float32)
+    picked = picked.astype(jnp.bfloat16).reshape(panels_here, per_panel, seg_here, width)
+    pick_mask = jnp.dot(chosen, valid.astype(jnp.bfloat16), preferred_element_type=jnp.float32)
+    pick_mask = pick_mask.astype(jnp.bfloat16).reshape(panels_here, per_panel, seg_here)
 
     def fetch(panel):
         return (
@@ -172,6 +175,7 @@
 
     s_copy(z, k).start()
 
+    out_ref[...] = jnp.zeros_like(out_ref)
     wide = lax.broadcasted_iota(jnp.int32, (q, width), 1)
     for seg in range(segs):
         wcols, vcols = [], []
@@ -245,7 +249,14 @@
             lo = pltpu.roll(low, (LANES - h * q) % LANES, 1) if h else low
             hi = pltpu.roll(high, (LANES + q - h * q) % LANES, 1) if h != 1 else high
             both = jnp.where(at < q, lo, hi)[:, : 2 * q]
-            out_ref[b, h * SRC_SHIFTS : (h + 1) * SRC_SHIFTS] = both.reshape(SRC_SHIFTS, per, 2 * q)
+            both = both.reshape(SRC_SHIFTS, per, 2 * q)
+            for p in range(2):
+                channel = idx_ref[p * per : (p + 1) * per, : 2 * q]
+                held = (channel >= b * resident) & (channel < (b + 1) * resident)
+                at_lags = pl.ds(h * SRC_SHIFTS, SRC_SHIFTS)
+                at_rows = pl.ds(p * per, per)
+                before = out_ref[at_lags, at_rows, :]
+                out_ref[at_lags, at_rows, :] = jnp.where(held[None], both, before)
 
     def item(d, way):
         b = z + d * (2 * way - 1)
@@ -322,9 +333,9 @@
     vmem = pl.BlockSpec(memory_space=pltpu.VMEM)
     dma = pltpu.SemaphoreType.DMA
     f32, bf16 = jnp.float32, jnp.bfloat16
-    found = pl.pallas_call(
+    return pl.pallas_call(
         functools.partial(kernel, n_chan),
-        out_shape=jax.ShapeDtypeStruct((n_chan, LAGS, per, resident // 2), f32),
+        out_shape=jax.ShapeDtypeStruct((LAGS, panels * per, resident // 2), f32),
         in_specs=[vmem] * 3,
         out_specs=vmem,
         scratch_shapes=[
@@ -353,10 +364,6 @@
             collective_id=0, has_side_effects=True, vmem_limit_bytes=48 * 1024 * 1024
         ),
     )(x, idx, val)
-    owners = source_channel_index[:, 0] // resident
-    return jnp.concatenate(
-        [lax.dynamic_index_in_dim(found, owners[p], 0, keepdims=False) for p in range(panels)], axis=1
-    )
 
 
 def solution(mesh):

time: 48 us -> 42.1 us (0.88)
  between operations: 3.62 us -> 0.02 us
  local copies, waits for them, and re-layouts: 6.48 us -> 4.82 us
    squeeze x1 -> x0, local copies, waits for them, and re-layouts: 1.27 us -> none  [fast_body(): lax.dynamic_index_in_dim(found, owners[p], 0, keepdims=False)]
    concatenate x1 -> x0, other arithmetic: 1.07 us -> none  [fast_body(): jnp.concatenate([lax.dynamic_index_in_dim(found, owners[p], 0, keepdims=F...]
    convert_element_type x1, other arithmetic: 0.01 us -> 0.68 us  [fast_body(): valid.T.astype(jnp.float32)[:, :, None]]
    broadcast_in_dim x2, local copies, waits for them, and re-layouts: 0.16 us -> 0.83 us  [fast_body(): jnp.broadcast_to(source_channel_index.reshape(-1)[:, None], (panels * per...]
    slice x2 -> x0, local copies, waits for them, and re-layouts: 0.67 us -> none  [the longest x1 0.56 us: fast_body(): owners[p]]
    unnamed x7 -> x2, local copies, waits for them, and re-layouts: 4.28 us -> 3.9 us
where the time goes in v2:
time: 42.1 us; the launch traced here: 41.9 us
  Pallas kernels  36.4 us (86%)
  local copies, waits for them, and re-layouts  4.82 us (11%)
  other arithmetic  0.68 us (2%)
    pallas_call x1, Pallas kernels, fast_body(): pl.pallas_call(functools.partial(kernel, n_chan), out_shape=jax.ShapeDtyp...  36.4 us
    unnamed x2, local copies, waits for them, and re-layouts  3.9 us

profile of v2, /device:TPU:0, one launch (start us, length us, event | category | flops | bytes accessed | tf_op | source)
XLA Modules:
  0.0 41.9 jit_solution(15095909386036482433)
XLA Ops:
  0.0 0.8 %broadcast_in_dim.6 = s32[64]{0:T(128)S(1)} reshape(s32[2,32]{1,0:T(2,128)} %param.5) | data formatting | bytes 512 | tf_op jit(solution)/shard_map/broadcast_in_dim | solution.py:330
  0.8 0.7 %convert_bitcast_fusion = f32[2,128]{1,0:T(2,128)S(1)} fusion(s32[128,2]{0,1:T(2,128)} %param.4), kind=kLoop, calls=%fused_computation.1 | loop fusion | flops 256 | bytes 2048 | tf_op jit(solution)/shard_map/convert_element_type | solution.py:331
  1.4 0.1 broadcast_in_dim.14.idx_ref
  1.5 0.1 broadcast_in_dim.15.val_ref
  1.6 2.9 %copy.6 = bf16[128,2,4096]{2,0,1:T(8,128)(2,1)S(1)} copy(bf16[128,2,4096]{2,1,0:T(2,128)(2,1)} %param.3) | data formatting | bytes 4194304 | tf_op args[0]
  4.5 36.4 %shard_map.37 = f32[32,64,64]{2,1,0:T(8,128)S(1)} custom-call(bf16[2,128,4096]{2,1,0:T(8,128)(2,1)S(1)} %bitcast.5, s32[64,128]{1,0:T(8,128)S(1)} %broadcast_in_dim.14.idx_ref, f32[2,128,128]{2,1,0:T(8,128)S(1)} %broadcast_in_dim.15.val_ref), custom_call_target="tpu_custom_call" | custom-call | tf_op jit(solution)/shard_map/pallas_call | solution.py:336
  41.0 1.0 %copy.8 = f32[32,64,64]{2,1,0:T(8,128)} copy(f32[32,64,64]{2,1,0:T(8,128)S(1)} %shard_map.37) | data formatting | bytes 1048576

commit v3 on v2

--- a/solution.py
+++ b/solution.py
@@ -162,7 +162,7 @@
             sel, x_ref[k, :, t : t + tile], preferred_element_type=jnp.float32
         ).astype(jnp.bfloat16)
     slots[z, k, :, width:] = jnp.dot(
-        sel, val_ref[k].astype(jnp.bfloat16), preferred_element_type=jnp.float32
+        sel, val_ref[k].astype(jnp.float32).astype(jnp.bfloat16), preferred_element_type=jnp.float32
     ).astype(jnp.bfloat16)
 
     @pl.when(has_left)
@@ -183,7 +183,7 @@
             side = x if half == 0 else 1 - x
             first = pl.multiple_of(side * (2 * q) + k * q, q)
             rec = x_ref[seg, pl.ds(first, q), :].astype(jnp.float32)
-            flag = val_ref[seg, pl.ds(first, q), :]
+            flag = val_ref[seg, pl.ds(first, q), :].astype(jnp.float32)
             mean = jnp.sum(rec * rec, axis=1, keepdims=True) * (1.0 / width)
             w = flag / jnp.sqrt(mean + 1e-05)
             for h in range(REC_SHIFTS):
@@ -328,7 +328,7 @@
     panels, per = source_channel_index.shape
     x = jnp.transpose(traces, (1, 0, 2))
     idx = jnp.broadcast_to(source_channel_index.reshape(-1)[:, None], (panels * per, LANES))
-    val = jnp.broadcast_to(valid.T.astype(jnp.float32)[:, :, None], (segs, resident, LANES))
+    val = jnp.broadcast_to(valid.T[:, :, None], (segs, resident, LANES))
     rows = SRC_SHIFTS * per
     vmem = pl.BlockSpec(memory_space=pltpu.VMEM)
     dma = pltpu.SemaphoreType.DMA

time: 42.1 us -> 42.1 us (level)
  other arithmetic: 0.68 us -> 0 us
  local copies, waits for them, and re-layouts: 4.82 us -> 5.5 us
    convert_element_type x1 -> x0, other arithmetic: 0.68 us -> none  [fast_body(): valid.T.astype(jnp.float32)[:, :, None]]
    broadcast_in_dim x1, local copies, waits for them, and re-layouts: 0.09 us -> 0.77 us  [fast_body(): val = jnp.broadcast_to(valid.T[:, :, None], (segs, resident, LANES))]
where the time goes in v3:
time: 42.1 us; the launch traced here: 41.9 us
  Pallas kernels  36.4 us (86%)
  local copies, waits for them, and re-layouts  5.5 us (13%)
    pallas_call x1, Pallas kernels, fast_body(): pl.pallas_call(functools.partial(kernel, n_chan), out_shape=jax.ShapeDtyp...  36.4 us
    unnamed x2, local copies, waits for them, and re-layouts  3.9 us

profile of v3, /device:TPU:0, one launch (start us, length us, event | category | flops | bytes accessed | tf_op | source)
XLA Modules:
  0.0 41.9 jit_solution(5911507386093791433)
XLA Ops:
  0.0 0.8 %broadcast_in_dim.6 = s32[64]{0:T(128)S(1)} reshape(s32[2,32]{1,0:T(2,128)} %param.5) | data formatting | bytes 512 | tf_op jit(solution)/shard_map/broadcast_in_dim | solution.py:330
  0.8 0.1 broadcast_in_dim.14.idx_ref
  0.8 0.8 %broadcast_in_dim.15.val_ref = s32[2,128,128]{2,1,0:T(8,128)S(1)} broadcast(s32[2,128]{1,0:T(2,128)} %bitcast.5), dimensions={0,1} | broadcast | bytes 132096 | tf_op jit(solution)/shard_map/broadcast_in_dim | solution.py:331
  1.6 2.9 %copy.6 = bf16[128,2,4096]{2,0,1:T(8,128)(2,1)S(1)} copy(bf16[128,2,4096]{2,1,0:T(2,128)(2,1)} %param.3) | data formatting | bytes 4194304 | tf_op args[0]
  4.5 36.4 %shard_map.37 = f32[32,64,64]{2,1,0:T(8,128)S(1)} custom-call(bf16[2,128,4096]{2,1,0:T(8,128)(2,1)S(1)} %bitcast.4, s32[64,128]{1,0:T(8,128)S(1)} %broadcast_in_dim.14.idx_ref, s32[2,128,128]{2,1,0:T(8,128)S(1)} %broadcast_in_dim.15.val_ref), custom_call_target="tpu_custom_call" | custom-call | tf_op jit(solution)/shard_map/pallas_call | solution.py:336
  41.0 1.0 %copy.8 = f32[32,64,64]{2,1,0:T(8,128)} copy(f32[32,64,64]{2,1,0:T(8,128)S(1)} %shard_map.37) | data formatting | bytes 1048576

commit v4 on v2

--- a/solution.py
+++ b/solution.py
@@ -11,6 +11,7 @@
 LAGS = 32
 SRC_SHIFTS = 8
 REC_SHIFTS = LAGS // SRC_SHIFTS
+PIECES = 2
 LANES = 128
 MESH = pl.DeviceIdType.MESH
 
@@ -102,7 +103,8 @@
     idx_sems, z_send, z_recv, s_send, s_recv, x_send, x_recv, f_send, f_recv,
 ):
     segs, resident, width = x_ref.shape
-    per = idx_ref.shape[0] // 2
+    panel = idx_ref.shape[0] // 2
+    per = panel // PIECES
     q = resident // 4
     z = lax.axis_index("chan")
     x = lax.axis_index("tm")
@@ -149,31 +151,35 @@
     idx_copy.start()
     idx_copy.wait()
 
-    lane = lax.broadcasted_iota(jnp.int32, (per, resident), 1)
-    sel = jnp.zeros((per, resident), jnp.float32)
+    lane = lax.broadcasted_iota(jnp.int32, (panel, resident), 1)
+    sel = jnp.zeros((panel, resident), jnp.float32)
     for ref in (idx_ref, idx_sib):
         for p in range(2):
-            hit = ref[p * per : (p + 1) * per, :] - z * resident == lane
+            hit = ref[p * panel : (p + 1) * panel, :] - z * resident == lane
             sel = sel + jnp.where(hit, 1.0, 0.0)
     sel = sel.astype(jnp.bfloat16)
     tile = 1024
+    def place(rows, at):
+        rows = rows.astype(jnp.bfloat16)
+        for piece in range(PIECES):
+            slots[z * PIECES + piece, k, :, at : at + rows.shape[1]] = rows[piece * per : (piece + 1) * per]
+
     for t in range(0, width, tile):
-        slots[z, k, :, t : t + tile] = jnp.dot(
-            sel, x_ref[k, :, t : t + tile], preferred_element_type=jnp.float32
-        ).astype(jnp.bfloat16)
-    slots[z, k, :, width:] = jnp.dot(
-        sel, val_ref[k].astype(jnp.bfloat16), preferred_element_type=jnp.float32
-    ).astype(jnp.bfloat16)
-
-    @pl.when(has_left)
-    def _():
-        z_copy(z, False).start()
-
-    @pl.when(has_right)
-    def _():
-        z_copy(z, True).start()
-
-    s_copy(z, k).start()
+        place(jnp.dot(sel, x_ref[k, :, t : t + tile], preferred_element_type=jnp.float32), t)
+    place(jnp.dot(sel, val_ref[k].astype(jnp.bfloat16), preferred_element_type=jnp.float32), width)
+
+    for piece in range(PIECES):
+        i = z * PIECES + piece
+
+        @pl.when(has_left)
+        def _(i=i):
+            z_copy(i, False).start()
+
+        @pl.when(has_right)
+        def _(i=i):
+            z_copy(i, True).start()
+
+        s_copy(i, k).start()
 
     out_ref[...] = jnp.zeros_like(out_ref)
     wide = lax.broadcasted_iota(jnp.int32, (q, width), 1)
@@ -240,6 +246,8 @@
 
     def final(b):
         f_copy(b).wait_recv()
+        block = b // PIECES
+        first = pl.multiple_of((b % PIECES) * per, per)
         rows = SRC_SHIFTS * per
         mine, other = fin[b], finr[b]
         low = jnp.where(k == 0, mine, other)
@@ -251,24 +259,25 @@
             both = jnp.where(at < q, lo, hi)[:, : 2 * q]
             both = both.reshape(SRC_SHIFTS, per, 2 * q)
             for p in range(2):
-                channel = idx_ref[p * per : (p + 1) * per, : 2 * q]
-                held = (channel >= b * resident) & (channel < (b + 1) * resident)
+                channel = idx_ref[pl.ds(p * panel + first, per), :][:, : 2 * q]
+                held = (channel >= block * resident) & (channel < (block + 1) * resident)
                 at_lags = pl.ds(h * SRC_SHIFTS, SRC_SHIFTS)
-                at_rows = pl.ds(p * per, per)
+                at_rows = pl.ds(p * panel + first, per)
                 before = out_ref[at_lags, at_rows, :]
                 out_ref[at_lags, at_rows, :] = jnp.where(held[None], both, before)
 
-    def item(d, way):
-        b = z + d * (2 * way - 1)
-        ok = (b >= 0) & (b < n_chan) & (d >= 0) & ((d > 0) | (way == 0))
-        return b, ok
-
-    @pl.loop(0, n_chan + 2)
+    def item(e, way):
+        d = (e + PIECES) // PIECES - 1
+        block = z + d * (2 * way - 1)
+        ok = (block >= 0) & (block < n_chan) & (d >= 0) & ((d > 0) | (way == 0))
+        return block * PIECES + (e + PIECES) % PIECES, ok
+
+    @pl.loop(0, n_chan * PIECES + 2)
     def _(d):
         from_left, ok_left = item(d, 0)
         from_right, ok_right = item(d, 1)
 
-        @pl.when(ok_left & (d > 0))
+        @pl.when(ok_left & (d >= PIECES))
         def _():
             z_copy(from_left, True).wait_recv()
 
@@ -278,7 +287,7 @@
 
             s_copy(from_left, k).start()
 
-        @pl.when(ok_right & (d > 0))
+        @pl.when(ok_right & (d >= PIECES))
         def _():
             z_copy(from_right, False).wait_recv()
 
@@ -308,13 +317,15 @@
             def _():
                 final(b2)
 
-    @pl.loop(0, n_chan)
+    @pl.loop(0, n_chan * PIECES)
     def _(b):
-        @pl.when(has_left & (b >= z))
+        block = b // PIECES
+
+        @pl.when(has_left & (block >= z))
         def _():
             z_copy(b, False).wait_send()
 
-        @pl.when(has_right & (b <= z))
+        @pl.when(has_right & (block <= z))
         def _():
             z_copy(b, True).wait_send()
 
@@ -326,10 +337,11 @@
 def fast_body(n_chan, traces, valid, source_channel_index):
     resident, segs, width = traces.shape
     panels, per = source_channel_index.shape
+    part, items = per // PIECES, n_chan * PIECES
     x = jnp.transpose(traces, (1, 0, 2))
     idx = jnp.broadcast_to(source_channel_index.reshape(-1)[:, None], (panels * per, LANES))
     val = jnp.broadcast_to(valid.T.astype(jnp.float32)[:, :, None], (segs, resident, LANES))
-    rows = SRC_SHIFTS * per
+    rows = SRC_SHIFTS * part
     vmem = pl.BlockSpec(memory_space=pltpu.VMEM)
     dma = pltpu.SemaphoreType.DMA
     f32, bf16 = jnp.float32, jnp.bfloat16
@@ -339,26 +351,26 @@
         in_specs=[vmem] * 3,
         out_specs=vmem,
         scratch_shapes=[
-            pltpu.VMEM((n_chan, segs, per, width + LANES), bf16),
+            pltpu.VMEM((items, segs, part, width + LANES), bf16),
             pltpu.VMEM((panels * per, LANES), jnp.int32),
             pltpu.VMEM((segs, 2 * LANES, width), bf16),
             pltpu.VMEM((segs, rows, width), bf16),
-            pltpu.VMEM((segs, per, 2 * LANES), f32),
-            pltpu.VMEM((segs, per, 2 * LANES), f32),
-            pltpu.VMEM((n_chan, rows + per, LANES), f32),
-            pltpu.VMEM((n_chan, rows + per, LANES), f32),
-            pltpu.VMEM((n_chan, rows + per, LANES), f32),
-            pltpu.VMEM((n_chan, rows, LANES), f32),
-            pltpu.VMEM((n_chan, rows, LANES), f32),
+            pltpu.VMEM((segs, part, 2 * LANES), f32),
+            pltpu.VMEM((segs, part, 2 * LANES), f32),
+            pltpu.VMEM((items, rows + part, LANES), f32),
+            pltpu.VMEM((items, rows + part, LANES), f32),
+            pltpu.VMEM((items, rows + part, LANES), f32),
+            pltpu.VMEM((items, rows, LANES), f32),
+            pltpu.VMEM((items, rows, LANES), f32),
             dma((2,)),
-            dma((n_chan, 2)),
-            dma((n_chan,)),
-            dma((n_chan,)),
-            dma((n_chan,)),
-            dma((n_chan,)),
-            dma((n_chan,)),
-            dma((n_chan,)),
-            dma((n_chan,)),
+            dma((items, 2)),
+            dma((items,)),
+            dma((items,)),
+            dma((items,)),
+            dma((items,)),
+            dma((items,)),
+            dma((items,)),
+            dma((items,)),
         ],
         compiler_params=pltpu.CompilerParams(
             collective_id=0, has_side_effects=True, vmem_limit_bytes=48 * 1024 * 1024

time: 42.1 us -> 42 us (level)
  no operation moved by 1% of the time
where the time goes in v4:
time: 42 us; the launch traced here: 41.9 us
  Pallas kernels  36.3 us (86%)
  local copies, waits for them, and re-layouts  4.82 us (11%)
  other arithmetic  0.68 us (2%)
    pallas_call x1, Pallas kernels, fast_body(): pl.pallas_call(functools.partial(kernel, n_chan), out_shape=jax.ShapeDtyp...  36.3 us
    unnamed x2, local copies, waits for them, and re-layouts  3.9 us

profile of v4, /device:TPU:0, one launch (start us, length us, event | category | flops | bytes accessed | tf_op | source)
XLA Modules:
  0.0 41.9 jit_solution(304861685702589187)
XLA Ops:
  0.0 0.8 %broadcast_in_dim.6 = s32[64]{0:T(128)S(1)} reshape(s32[2,32]{1,0:T(2,128)} %param.5) | data formatting | bytes 512 | tf_op jit(solution)/shard_map/broadcast_in_dim | solution.py:342
  0.8 0.7 %convert_bitcast_fusion = f32[2,128]{1,0:T(2,128)S(1)} fusion(s32[128,2]{0,1:T(2,128)} %param.4), kind=kLoop, calls=%fused_computation.1 | loop fusion | flops 256 | bytes 2048 | tf_op jit(solution)/shard_map/convert_element_type | solution.py:343
  1.4 0.1 broadcast_in_dim.14.idx_ref
  1.5 0.1 broadcast_in_dim.15.val_ref
  1.6 2.9 %copy.6 = bf16[128,2,4096]{2,0,1:T(8,128)(2,1)S(1)} copy(bf16[128,2,4096]{2,1,0:T(2,128)(2,1)} %param.3) | data formatting | bytes 4194304 | tf_op args[0]
  4.5 36.3 %shard_map.37 = f32[32,64,64]{2,1,0:T(8,128)S(1)} custom-call(bf16[2,128,4096]{2,1,0:T(8,128)(2,1)S(1)} %bitcast.5, s32[64,128]{1,0:T(8,128)S(1)} %broadcast_in_dim.14.idx_ref, f32[2,128,128]{2,1,0:T(8,128)S(1)} %broadcast_in_dim.15.val_ref), custom_call_target="tpu_custom_call" | custom-call | tf_op jit(solution)/shard_map/pallas_call | solution.py:348
  40.9 1.0 %copy.8 = f32[32,64,64]{2,1,0:T(8,128)} copy(f32[32,64,64]{2,1,0:T(8,128)S(1)} %shard_map.37) | data formatting | bytes 1048576

commit v5 on v4

--- a/solution.py
+++ b/solution.py
@@ -192,15 +192,16 @@
             flag = val_ref[seg, pl.ds(first, q), :]
             mean = jnp.sum(rec * rec, axis=1, keepdims=True) * (1.0 / width)
             w = flag / jnp.sqrt(mean + 1e-05)
+            turned = []
             for h in range(REC_SHIFTS):
                 by = SRC_SHIFTS * h
                 moved = rec
                 if by:
                     moved = jnp.where(wide < width - by, pltpu.roll(rec, width - by, 1), 0.0)
-                row = (half * REC_SHIFTS + h) * q
-                shifted_rec[seg, row : row + q, :] = moved.astype(jnp.bfloat16)
+                turned.append(moved.astype(jnp.bfloat16))
                 wcols.append(w)
                 vcols.append(flag)
+            shifted_rec[seg, :, half * LANES : (half + 1) * LANES] = jnp.concatenate(turned, axis=0).T
         wrow[seg] = jnp.concatenate(wcols, axis=0).T[:per]
         vrow[seg] = jnp.concatenate(vcols, axis=0).T[:per]
 
@@ -221,7 +222,7 @@
                     moved = jnp.where(wide[:per] >= j, pltpu.roll(src, j, 1), 0.0)
                 shifted_src[seg, j * per : (j + 1) * per, :] = moved.astype(jnp.bfloat16)
             d = lax.dot_general(
-                shifted_src[seg], shifted_rec[seg], (((1,), (1,)), ((), ())),
+                shifted_src[seg], shifted_rec[seg], (((1,), (0,)), ((), ())),
                 preferred_element_type=jnp.float32,
             )
             term = d.reshape(SRC_SHIFTS, per, 2 * LANES) * (a * wrow[seg])[None]
@@ -353,7 +354,7 @@
         scratch_shapes=[
             pltpu.VMEM((items, segs, part, width + LANES), bf16),
             pltpu.VMEM((panels * per, LANES), jnp.int32),
-            pltpu.VMEM((segs, 2 * LANES, width), bf16),
+            pltpu.VMEM((segs, width, 2 * LANES), bf16),
             pltpu.VMEM((segs, rows, width), bf16),
             pltpu.VMEM((segs, part, 2 * LANES), f32),
             pltpu.VMEM((segs, part, 2 * LANES), f32),

time: 42 us -> 40.4 us (0.962)
  Pallas kernels: 36.3 us -> 34.7 us
    pallas_call x1, Pallas kernels: 36.3 us -> 34.7 us  [fast_body(): pl.pallas_call(functools.partial(kernel, n_chan), out_shape=jax.ShapeDtyp...]
where the time goes in v5:
time: 40.4 us; the launch traced here: 40.3 us
  Pallas kernels  34.7 us (86%)
  local copies, waits for them, and re-layouts  4.82 us (12%)
  other arithmetic  0.68 us (2%)
    pallas_call x1, Pallas kernels, fast_body(): pl.pallas_call(functools.partial(kernel, n_chan), out_shape=jax.ShapeDtyp...  34.7 us
    unnamed x2, local copies, waits for them, and re-layouts  3.9 us
    broadcast_in_dim x2, local copies, waits for them, and re-layouts, fast_body(): jnp.broadcast_to(source_channel_index.reshape(-1)[:, None], (panels * per...  0.83 us

profile of v5, /device:TPU:0, one launch (start us, length us, event | category | flops | bytes accessed | tf_op | source)
XLA Modules:
  0.0 40.3 jit_solution(12453420338954592107)
XLA Ops:
  0.0 0.8 %broadcast_in_dim.6 = s32[64]{0:T(128)S(1)} reshape(s32[2,32]{1,0:T(2,128)} %param.5) | data formatting | bytes 512 | tf_op jit(solution)/shard_map/broadcast_in_dim | solution.py:343
  0.8 0.7 %convert_bitcast_fusion = f32[2,128]{1,0:T(2,128)S(1)} fusion(s32[128,2]{0,1:T(2,128)} %param.4), kind=kLoop, calls=%fused_computation.1 | loop fusion | flops 256 | bytes 2048 | tf_op jit(solution)/shard_map/convert_element_type | solution.py:344
  1.4 0.1 broadcast_in_dim.14.idx_ref
  1.5 0.1 broadcast_in_dim.15.val_ref
  1.6 2.9 %copy.6 = bf16[128,2,4096]{2,0,1:T(8,128)(2,1)S(1)} copy(bf16[128,2,4096]{2,1,0:T(2,128)(2,1)} %param.3) | data formatting | bytes 4194304 | tf_op args[0]
  4.5 34.7 %shard_map.37 = f32[32,64,64]{2,1,0:T(8,128)S(1)} custom-call(bf16[2,128,4096]{2,1,0:T(8,128)(2,1)S(1)} %bitcast.5, s32[64,128]{1,0:T(8,128)S(1)} %broadcast_in_dim.14.idx_ref, f32[2,128,128]{2,1,0:T(8,128)S(1)} %broadcast_in_dim.15.val_ref), custom_call_target="tpu_custom_call" | custom-call | tf_op jit(solution)/shard_map/pallas_call | solution.py:349
  39.3 1.0 %copy.8 = f32[32,64,64]{2,1,0:T(8,128)} copy(f32[32,64,64]{2,1,0:T(8,128)S(1)} %shard_map.37) | data formatting | bytes 1048576
